TPU v7x, 128 devices: a whole 4x4x4 slice. The times are simulated.
128 devices in a mesh: dp: 8 (over y, core), tensor: 16 (over z, x).
Axes of the slice: x: 4, y: 4, z: 4, core: 2. Of those that a mesh axis runs over, the one named last changes fastest.
Arguments:
- hidden: bfloat16 [1024, 53248], P('dp', 'tensor'), may hold values from -6 to 6
- exponents: int32 [1024], P('dp'), may hold values from -3 to 0
- weight_levels: bfloat16 [53248, 16384], P('tensor', 'dp'), may hold values from -8 to 7
- column_scale: float32 [16384], P('dp'), may hold values from 0.00043335953 to 0.0043335953
- residual: bfloat16 [1024, 16384], P('tensor', 'dp'), may hold values from -6 to 6
Outputs:
- layer_output: bfloat16 [1024, 16384], P('tensor', 'dp')
All inputs are finite; a program needn't handle non-finite values.
Results may differ from a plain program's by a relative error of at most 0.018.
Values may be sent and summed in bfloat16 or wider, within the bound.
A program may use at most 128 MiB of HBM per device.

v0:
```python
import math

import jax
import jax.numpy as jnp
import numpy as np
from jax import lax
from jax.sharding import PartitionSpec as P

FF = 53248
HAD_SMALL = 52


def partner_2(value, axis, bit):
    mask = 2**bit
    pairs = [(source, source ^ mask) for source in range(lax.axis_size(axis))]
    return lax.ppermute(value, axis, pairs)


def paley_table():
    members = [(a, b) for a in range(5) for b in range(5)]
    squares = set()
    for a, b in members:
        if (a, b) != (0, 0):
            squares.add(((a * a + 2 * b * b) % 5, 2 * a * b % 5))
    field_size = len(members)
    jacobsthal = np.zeros((field_size, field_size))
    for i, (a, b) in enumerate(members):
        for j, (c, d) in enumerate(members):
            difference = ((a - c) % 5, (b - d) % 5)
            if difference == (0, 0):
                jacobsthal[i, j] = 0.0
            elif difference in squares:
                jacobsthal[i, j] = 1.0
            else:
                jacobsthal[i, j] = -1.0
    conference = np.zeros((field_size + 1, field_size + 1))
    conference[0, 1:] = 1.0
    conference[1:, 0] = 1.0
    conference[1:, 1:] = jacobsthal
    hadamard = np.kron(conference, np.array([[1.0, -1.0], [-1.0, -1.0]]))
    hadamard = hadamard + np.kron(np.eye(field_size + 1), np.array([[1.0, 1.0], [1.0, -1.0]]))
    return hadamard


def sylvester(count):
    positions = jnp.arange(count, dtype=jnp.int32)
    common = jnp.bitwise_and(positions[:, None], positions[None, :])
    parity = jnp.zeros((count, count), jnp.int32)
    for offset in range(count.bit_length()):
        parity = parity + jnp.bitwise_and(jnp.right_shift(common, offset), 1)
    return (1 - 2 * jnp.bitwise_and(parity, 1)).astype(jnp.float32)


def shards(hidden, exponents, weight_levels, column_scale, residual):
    local_rows = hidden.shape[0]
    local_width = hidden.shape[1]
    local_blocks = local_width // HAD_SMALL
    tensor_count = lax.axis_size("tensor")
    small_table = jnp.asarray(paley_table(), dtype=jnp.float32)
    inner_table = sylvester(local_blocks)
    rotated = hidden.astype(jnp.float32).T.reshape(local_blocks, HAD_SMALL, local_rows)
    rotated = jnp.einsum("jkr,kb->jbr", rotated, small_table, precision=lax.Precision.HIGHEST)
    rotated = jnp.einsum("jbr,ja->abr", rotated, inner_table, precision=lax.Precision.HIGHEST)
    position = lax.axis_index("tensor")
    for bit_number in range(tensor_count.bit_length() - 1):
        partner = partner_2(rotated, "tensor", bit_number)
        upper_half = jnp.bitwise_and(jnp.right_shift(position, bit_number), 1) == 1
        rotated = jnp.where(upper_half, partner - rotated, partner + rotated)
    rotated = rotated * (1.0 / math.sqrt(FF))
    powers = jnp.exp2(exponents.astype(jnp.float32))
    inverse = jnp.exp2(-exponents.astype(jnp.float32))
    code_values = jnp.clip(rotated * inverse[None, None, :], -8.0, 7.0).astype(jnp.bfloat16)
    dequant = code_values * powers.astype(jnp.bfloat16)[None, None, :]
    flat_rows = dequant.reshape(local_width, local_rows).T
    partial_value = jnp.dot(
        lax.all_gather(flat_rows, "dp", axis=0, tiled=True),
        weight_levels,
        preferred_element_type=jnp.float32,
    )
    totals = lax.psum_scatter(
        partial_value.astype(jnp.bfloat16), "tensor", scatter_dimension=0, tiled=True
    ).astype(jnp.float32)
    return (totals * column_scale[None, :] + residual.astype(jnp.float32)).astype(jnp.bfloat16)


def solution(mesh):
    return jax.shard_map(
        shards,
        mesh=mesh,
        in_specs=(P("dp", "tensor"), P("dp"), P("tensor", "dp"), P("dp"), P("tensor", "dp")),
        out_specs=P("tensor", "dp"),
        check_vma=False,
    )
```

profile of v0, /device:TPU:0, one launch (start us, length us, event | category | flops | bytes accessed | tf_op | source)
XLA Modules:
  0.0 329.7 jit_solution(12119764068237406566)
XLA Ops:
  6.5 0.0 all-gather.2.cloned.1.call-start
  6.5 1.5 copy.7
  8.1 0.1 reshape.9
  8.2 0.0 copy-done.2
  8.3 0.9 fusion.46
  9.2 1.7 fusion
  10.9 1.7 collective-permute-start
  12.6 37.3 %collective-permute-done = f32[64,52,128]{2,0,1:T(8,128)} collective-permute-done((f32[64,52,128]{2,0,1:T(8,128)S(1)}, f32[64,52,128]{2,0,1:T(8,128)}, u32[]{:S(2)}, u32[]{:S(2)}) %collective-permute-start) | collective-permute-done | bytes 1703968 | tf_op jit(solution)/shard_map/ppermute | solution.py:16
  49.9 1.8 add_select_fusion.2
  51.7 0.0 copy-start
  51.7 3.4 %collective-permute-start.1 = (f32[64,52,128]{2,0,1:T(8,128)S(1)}, f32[64,52,128]{2,0,1:T(8,128)S(1)}, u32[]{:S(2)}, u32[]{:S(2)}) collective-permute-start(f32[64,52,128]{2,0,1:T(8,128)S(1)} %add_select_fusion.2), channel_id=1, source_target_pairs={{0,2},{1,3},{2,0},{3,1},{4,6},{5,7},{6,4},{7,5},{8,10},{9,11},{10,... | collective-permute-start | bytes 5111816 | tf_op jit(solution)/shard_map/ppermute | solution.py:16
  55.0 0.0 copy-done
  55.0 36.3 %collective-permute-done.1 = f32[64,52,128]{2,0,1:T(8,128)S(1)} collective-permute-done((f32[64,52,128]{2,0,1:T(8,128)S(1)}, f32[64,52,128]{2,0,1:T(8,128)S(1)}, u32[]{:S(2)}, u32[]{:S(2)}) %collective-permute-start.1) | collective-permute-done | bytes 1703968 | tf_op jit(solution)/shard_map/ppermute | solution.py:16
  91.4 1.8 add_select_fusion.1
  93.2 2.2 collective-permute-start.2
  95.4 35.5 %collective-permute-done.2 = f32[64,52,128]{2,0,1:T(8,128)} collective-permute-done((f32[64,52,128]{2,0,1:T(8,128)S(1)}, f32[64,52,128]{2,0,1:T(8,128)}, u32[]{:S(2)}, u32[]{:S(2)}) %collective-permute-start.2) | collective-permute-done | bytes 1703968 | tf_op jit(solution)/shard_map/ppermute | solution.py:16
  130.9 1.8 add_select_fusion
  132.8 3.8 %collective-permute-start.3 = (f32[64,52,128]{2,0,1:T(8,128)S(1)}, f32[64,52,128]{2,0,1:T(8,128)S(1)}, u32[]{:S(2)}, u32[]{:S(2)}) collective-permute-start(f32[64,52,128]{2,0,1:T(8,128)S(1)} %add_select_fusion), channel_id=1, source_target_pairs={{0,8},{1,9},{2,10},{3,11},{4,12},{5,13},{6,14},{7,15},{8,0},{9,1},... | collective-permute-start | bytes 5111816 | tf_op jit(solution)/shard_map/ppermute | solution.py:16
  136.5 0.0 copy-done.4
  136.5 34.5 %collective-permute-done.3 = f32[64,52,128]{2,0,1:T(8,128)S(1)} collective-permute-done((f32[64,52,128]{2,0,1:T(8,128)S(1)}, f32[64,52,128]{2,0,1:T(8,128)S(1)}, u32[]{:S(2)}, u32[]{:S(2)}) %collective-permute-start.3) | collective-permute-done | bytes 1703968 | tf_op jit(solution)/shard_map/ppermute | solution.py:16
  171.0 0.4 fusion.3
  171.4 0.6 copy.8
  172.0 1.1 reshape.10
  173.0 0.0 all-gather.2.cloned.1.call-update
  173.1 0.0 reduce-scatter.2.cloned.1.call-start
  173.1 49.0 %all-gather.2.cloned.1.call-done = bf16[1024,3328]{0,1:T(8,128)(2,1)} async-done(((bf16[128,3328]{0,1:T(8,128)(2,1)}), bf16[1024,3328]{0,1:T(8,128)(2,1)}) %all-gather.2.cloned.1.call-update) | async-done | bytes 6815760 | tf_op jit(solution)/shard_map/all_gather | solution.py:76
  222.1 20.0 %convolution_convert_fusion = bf16[1024,2048]{1,0:T(8,128)(2,1)} fusion(bf16[1024,3328]{0,1:T(8,128)(2,1)} %all-gather.2.cloned.1.call-done, bf16[3328,2048]{1,0:T(8,128)(2,1)} %param.8), kind=kOutput, calls=%fused_computation | convolution fusion | flops 13960740864 | bytes 24641536 | tf_op jit(solution)/shard_map/dot_general | solution.py:75
  242.1 0.0 reduce-scatter.2.cloned.1.call-update
  242.1 79.0 %reduce-scatter.2.cloned.1.call-done = bf16[64,2048]{1,0:T(8,128)(2,1)} async-done(((bf16[1024,2048]{1,0:T(8,128)(2,1)}), bf16[64,2048]{1,0:T(8,128)(2,1)}) %reduce-scatter.2.cloned.1.call-update) | async-done | bytes 262160 | tf_op jit(solution)/shard_map/reduce_scatter | solution.py:80
  321.1 0.0 copy-done.1
  321.1 0.0 copy-done.3
  321.1 1.7 add_convert_fusion
  (5 shorter events, 0.0 us)
Async XLA Ops:
  6.5 215.6 %all-gather.2.cloned.1.call-start = ((), (), s32[]{:S(2)}) async-start(), calls=%async_computation.1 | async-start | bytes 7667712 | tf_op jit(solution)/shard_map/all_gather | solution.py:76
  6.5 1.7 copy-start.2
  10.9 39.0 %collective-permute-start = (f32[64,52,128]{2,0,1:T(8,128)S(1)}, f32[64,52,128]{2,0,1:T(8,128)}, u32[]{:S(2)}, u32[]{:S(2)}) collective-permute-start(f32[64,52,128]{2,0,1:T(8,128)S(1)} %fusion), channel_id=1, source_target_pairs={{0,1},{1,0},{2,3},{3,2},{4,5},{5,4},{6,7},{7,6},{8,9},{9,8},{10,11... | collective-permute-start | bytes 5111816 | tf_op jit(solution)/shard_map/ppermute | solution.py:16
  51.7 3.4 %copy-start = (f32[64,52,128]{2,0,1:T(8,128)}, f32[64,52,128]{2,0,1:T(8,128)S(1)}, u32[]{:S(2)}) copy-start(f32[64,52,128]{2,0,1:T(8,128)S(1)} %add_select_fusion.2) | copy-start | bytes 5111812
  51.7 39.7 %collective-permute-start.1 = (f32[64,52,128]{2,0,1:T(8,128)S(1)}, f32[64,52,128]{2,0,1:T(8,128)S(1)}, u32[]{:S(2)}, u32[]{:S(2)}) collective-permute-start(f32[64,52,128]{2,0,1:T(8,128)S(1)} %add_select_fusion.2), channel_id=1, source_target_pairs={{0,2},{1,3},{2,0},{3,1},{4,6},{5,7},{6,4},{7,5},{8,10},{9,11},{10,... | collective-permute-start | bytes 5111816 | tf_op jit(solution)/shard_map/ppermute | solution.py:16
  93.2 37.8 %collective-permute-start.2 = (f32[64,52,128]{2,0,1:T(8,128)S(1)}, f32[64,52,128]{2,0,1:T(8,128)}, u32[]{:S(2)}, u32[]{:S(2)}) collective-permute-start(f32[64,52,128]{2,0,1:T(8,128)S(1)} %add_select_fusion.1), channel_id=1, source_target_pairs={{0,4},{1,5},{2,6},{3,7},{4,0},{5,1},{6,2},{7,3},{8,12},{9,13},{10,... | collective-permute-start | bytes 5111816 | tf_op jit(solution)/shard_map/ppermute | solution.py:16
  95.4 41.1 %copy-start.4 = (s32[128]{0:T(128)S(1)}, s32[128]{0:T(128)}, u32[]{:S(2)}) copy-start(s32[128]{0:T(128)} %param.7) | copy-start | bytes 1540
  132.8 38.2 %collective-permute-start.3 = (f32[64,52,128]{2,0,1:T(8,128)S(1)}, f32[64,52,128]{2,0,1:T(8,128)S(1)}, u32[]{:S(2)}, u32[]{:S(2)}) collective-permute-start(f32[64,52,128]{2,0,1:T(8,128)S(1)} %add_select_fusion), channel_id=1, source_target_pairs={{0,8},{1,9},{2,10},{3,11},{4,12},{5,13},{6,14},{7,15},{8,0},{9,1},... | collective-permute-start | bytes 5111816 | tf_op jit(solution)/shard_map/ppermute | solution.py:16
  173.1 148.1 %reduce-scatter.2.cloned.1.call-start = ((), (), s32[]{:S(2)}) async-start(), calls=%async_computation.2 | async-start | bytes 4456448 | tf_op jit(solution)/shard_map/reduce_scatter | solution.py:80
  242.1 79.0 %copy-start.1 = (bf16[64,2048]{1,0:T(8,128)(2,1)S(1)}, bf16[64,2048]{1,0:T(8,128)(2,1)}, u32[]{:S(2)}) copy-start(bf16[64,2048]{1,0:T(8,128)(2,1)} %param.10) | copy-start | bytes 786436
  242.1 79.0 %copy-start.3 = (f32[2048]{0:T(1024)S(1)}, f32[2048]{0:T(1024)}, u32[]{:S(2)}) copy-start(f32[2048]{0:T(1024)} %param.9) | copy-start | bytes 24580
Sparse Core Ops, SparseCore 0:
  173.2 48.9 all-gather.1
  242.3 78.8 reduce-scatter.1
where the time goes:
time: 330 us
  waiting for transfers between devices  272 us (82%)
  matrix products  22.6 us (7%)
  between operations  13.5 us (4%)
  starting transfers between devices  11.1 us (3%)
  other arithmetic  7.56 us (2%)
  local copies, waits for them, and re-layouts  3.32 us (1%)
    ppermute x4, waiting for transfers between devices, partner_2(): return lax.ppermute(value, axis, pairs)  144 us
    reduce_scatter x1, waiting for transfers between devices, shards(): lax.psum_scatter(partial_value.astype(jnp.bfloat16), 'tensor', scatter_di...  79 us
    all_gather x1, waiting for transfers between devices, shards(): lax.all_gather(flat_rows, 'dp', axis=0, tiled=True)  49 us
    dot_general x1, matrix products, shards(): jnp.dot(lax.all_gather(flat_rows, 'dp', axis=0, tiled=True), weight_level...  20 us
    ppermute x4, starting transfers between devices, partner_2(): return lax.ppermute(value, axis, pairs)  11 us
  transfers between devices with their start and end apart: 6, of which 6 were waited for; matrix products, arithmetic and copies ran while one was open for 0% of the time, Pallas kernels for 0%

commit v1 on v0

v1 whole, which is shorter than its diff:
```python
import math

import jax
import jax.numpy as jnp
import ml_dtypes
import numpy as np
from jax import lax
from jax.experimental import pallas as pl
from jax.experimental.pallas import tpu as pltpu
from jax.sharding import PartitionSpec as P

FF = 53248
HAD_SMALL = 52
WIDE = 1664
DP, TENSOR, RING = 8, 16, 4
ROWS = 128
WIDTH = 2 * WIDE
COLS = 2048
HALF = COLS // 2
CHUNKS = 4
PIECE = ROWS // CHUNKS
SUB = PIECE // 2
F32, BF16 = jnp.float32, jnp.bfloat16


def paley_table():
    members = [(a, b) for a in range(5) for b in range(5)]
    squares = set()
    for a, b in members:
        if (a, b) != (0, 0):
            squares.add(((a * a + 2 * b * b) % 5, 2 * a * b % 5))
    jacobsthal = np.zeros((25, 25))
    for i, (a, b) in enumerate(members):
        for j, (c, d) in enumerate(members):
            difference = ((a - c) % 5, (b - d) % 5)
            if difference != (0, 0):
                jacobsthal[i, j] = 1.0 if difference in squares else -1.0
    conference = np.zeros((26, 26))
    conference[0, 1:] = 1.0
    conference[1:, 0] = 1.0
    conference[1:, 1:] = jacobsthal
    hadamard = np.kron(conference, np.array([[1.0, -1.0], [-1.0, -1.0]]))
    return hadamard + np.kron(np.eye(26), np.array([[1.0, 1.0], [1.0, -1.0]]))


def sylvester(count):
    table = np.ones((1, 1))
    while table.shape[0] < count:
        table = np.kron(np.array([[1.0, 1.0], [1.0, -1.0]]), table)
    return table


def kernel(
    exponents, hidden_hbm, wide_hbm, weights_hbm, scale_hbm, residual_hbm, out,
    hidden, wide, weights, scale, residual,
    stage, got, stage_back, got_back, codes, sums,
    a1, a2, a3, a4, b1, b2, b3, b4,
    load_sem, out_send, out_recv, back_send, back_recv, own_sem,
    y_send, y_recv, pair_send, pair_recv, rs_send, rs_recv,
):
    d, t = lax.axis_index("dp"), lax.axis_index("tensor")
    z, x = lax.div(t, RING), lax.rem(t, RING)
    core = lax.rem(d, 2)

    def loads():
        pairs = [
            (hidden_hbm, hidden), (wide_hbm, wide), (weights_hbm, weights),
            (scale_hbm, scale), (residual_hbm, residual),
        ]
        return [pltpu.make_async_copy(src, dst, load_sem.at[i]) for i, (src, dst) in enumerate(pairs)]

    for load in loads():
        load.start()

    def dp_device(distance):
        return (lax.rem(d + 2 * distance + DP, DP), t)

    def pair_device():
        return (d + 1 - 2 * core, t)

    def plane_device(dz, dx):
        return (d, lax.rem(z + dz + RING, RING) * RING + lax.rem(x + dx + RING, RING))

    def offset_device(off):
        return plane_device(lax.div(off, RING), lax.rem(off, RING))

    def offset_source(off):
        return plane_device(-lax.div(off, RING), -lax.rem(off, RING))

    barrier = pltpu.get_barrier_semaphore()

    def greet(off, carry):
        pl.semaphore_signal(barrier, inc=1, device_id=offset_device(off), device_id_type=pl.DeviceIdType.MESH)
        return carry

    lax.fori_loop(1, TENSOR, greet, 0)
    for device in (dp_device(1), dp_device(-1), pair_device()):
        pl.semaphore_signal(barrier, inc=1, device_id=device, device_id_type=pl.DeviceIdType.MESH)

    def remote(src, dst, send, recv, device):
        return pltpu.make_async_remote_copy(
            src_ref=src, dst_ref=dst, send_sem=send, recv_sem=recv,
            device_id=device, device_id_type=pl.DeviceIdType.MESH,
        )

    loads()[0].wait()

    def split(pair, carry):
        at = pl.multiple_of(pair * 16, 16)
        block = hidden[pl.ds(at, 16), :].astype(F32)
        for i in range(2):
            rows = block[8 * i : 8 * i + 8]
            stage[2 * pair + i] = jnp.concatenate([rows[:, :WIDE], rows[:, WIDE:]], axis=0).astype(BF16)
        return carry

    lax.fori_loop(0, ROWS // 16, split, 0)
    pl.semaphore_wait(barrier, TENSOR - 1 + 3)

    def exchange(source, target, send, recv, own):
        def make(off):
            device = offset_device(off)
            return remote(source.at[device[1]], target.at[t], send.at[off], recv.at[off], device)

        def begin(off, carry):
            make(off).start()
            return carry

        def finish(off, carry):
            sender = offset_source(off)[1]
            remote(source.at[t], target.at[sender], send.at[off], recv.at[off], offset_device(off)).wait_recv()
            return carry

        def drain(off, carry):
            make(off).wait_send()
            return carry

        mine = pltpu.make_async_copy(source.at[t], target.at[t], own)
        mine.start()
        lax.fori_loop(1, TENSOR, begin, 0)

        def wait():
            mine.wait()
            lax.fori_loop(1, TENSOR, finish, 0)

        return wait, lambda: lax.fori_loop(1, TENSOR, drain, 0)

    out_wait, out_drain = exchange(stage, got, out_send, out_recv, own_sem.at[0])
    out_wait()
    loads()[1].wait()

    row = lax.broadcasted_iota(jnp.int32, (8, 1), 0)
    exponent = jnp.zeros((8, 1), jnp.int32)
    for r in range(8):
        exponent = jnp.where(row == r, exponents[t * 8 + r], exponent)
    power = jnp.left_shift(1, exponent + 3).astype(F32) * 0.125
    low, high = power * -8.0, power * 7.0

    def transform(at, size):
        left = got[...].reshape(TENSOR * 16, WIDE)
        product = jnp.dot(left, wide[:, pl.ds(at, size)], preferred_element_type=F32)
        parts = [product[8 * i : 8 * i + 8] for i in range(2 * TENSOR)]
        step = 1
        while step < len(parts):
            for i in range(len(parts)):
                if i & step == 0:
                    u, v = parts[i], parts[i + step]
                    parts[i], parts[i + step] = u + v, u - v
            step *= 2
        parts = [jnp.minimum(jnp.maximum(p * (1.0 / math.sqrt(FF)), low), high) for p in parts]
        for i in range(TENSOR):
            stage_back[i, :, pl.ds(at, size)] = jnp.concatenate(parts[2 * i : 2 * i + 2], axis=0).astype(BF16)

    def transform_step(i, carry):
        transform(pl.multiple_of(i * 256, 256), 256)
        return carry

    lax.fori_loop(0, WIDE // 256, transform_step, 0)
    transform(WIDE // 256 * 256, WIDE % 256)

    back_wait, back_drain = exchange(stage_back, got_back, back_send, back_recv, own_sem.at[1])
    out_drain()
    back_wait()

    for chunk in range(CHUNKS):
        for side in range(2):
            first = side * (TENSOR // 2) + 2 * chunk
            blocks = [got_back[first + i].astype(F32) for i in range(2)]
            for half in range(2):
                rows = jnp.concatenate([b[8 * half : 8 * half + 8] for b in blocks], axis=0)
                codes[chunk, d, side * SUB : side * SUB + SUB, half * WIDE : half * WIDE + WIDE] = rows.astype(BF16)
    back_drain()

    def index(distance):
        return lax.rem(d + 2 * distance + DP, DP)

    def whole(chunk, distance):
        return codes.at[chunk, index(distance)]

    def part(chunk, distance, side):
        return codes.at[chunk, index(distance), side * SUB : side * SUB + SUB]

    def y_copy(chunk, kind, receiving):
        sign = 1 if kind in (0, 2) else -1
        if kind < 2:
            ref = whole(chunk, -sign if receiving else 0)
        else:
            ref = part(chunk, -2 * sign if receiving else -sign, kind - 2)
        return remote(ref, ref, y_send.at[chunk, kind], y_recv.at[chunk, kind], dp_device(sign))

    def pair_copy(chunk, kind, receiving):
        def ref_of(base):
            if kind < 3:
                return codes.at[chunk, lax.rem(base + 2 * (0, -1, 1)[kind] + DP, DP)]
            return codes.at[chunk, lax.rem(base + 4, DP), (kind - 3) * SUB : (kind - 3) * SUB + SUB]

        ref = ref_of(pair_device()[0] if receiving else d)
        return remote(ref, ref, pair_send.at[chunk, kind], pair_recv.at[chunk, kind], pair_device())

    def send_own(chunk):
        for kind in range(2):
            y_copy(chunk, kind, False).start()
        pair_copy(chunk, 0, False).start()

    lanes = (slice(0, HALF), slice(HALF, COLS))
    bufs = ((a1, a2, a3, a4), (b1, b2, b3, b4))

    def group(chunk, path, target, side=None):
        span = slice(None) if side is None else slice(2 * side, 2 * side + 2)
        if path == 0:
            return (chunk, target, span, slice(None), lanes[path])
        return (chunk, span, target, slice(None), lanes[path])

    def block(chunk, path, target, side=None):
        width = HALF if side is None else HALF // 2
        begin = lanes[path].start + (0 if side is None else side * width)
        where = (z, target) if path == 0 else (target, x)
        return (chunk, *where, slice(None), slice(begin, begin + width))

    def axes(path, phase):
        along_z = (path == 0) == (phase == 0)
        if along_z:
            return z, lambda n: plane_device(n, 0)
        return x, lambda n: plane_device(0, n)

    def rs_copy(chunk, path, step, way):
        sign = 1 if way == 0 else -1
        here, device = axes(path, step // 2)
        pick = group if step < 2 else block
        if step % 2 == 0:
            src = sums.at[pick(chunk, path, lax.rem(here + 2, RING), way)]
        else:
            src = sums.at[pick(chunk, path, lax.rem(here + sign + RING, RING))]
        number = (path * 4 + step) * 2 + way
        return remote(
            src, bufs[path][step].at[chunk, way],
            rs_send.at[chunk, number], rs_recv.at[chunk, number], device(sign),
        )

    def rs_start(chunk, path, step):
        for way in range(2):
            rs_copy(chunk, path, step, way).start()

    def rs_wait(chunk, path, step):
        for way in range(2):
            rs_copy(chunk, path, step, way).wait_recv()

    def add_into(where, buffer):
        sums[where] = (sums[where].astype(F32) + buffer.astype(F32)).astype(BF16)

    def rs_second(chunk, path, phase):
        step = 2 * phase
        pick = group if phase == 0 else block
        here, _ = axes(path, phase)
        for way in range(2):
            sign = 1 if way == 0 else -1
            rs_copy(chunk, path, step, way).wait_recv()
            add_into(pick(chunk, path, lax.rem(here + sign + RING, RING), way), bufs[path][step][chunk, way])
            rs_copy(chunk, path, step + 1, way).start()

    def rs_third(chunk, path):
        rs_wait(chunk, path, 1)
        here, _ = axes(path, 0)
        where = group(chunk, path, here)
        buffer = bufs[path][1]
        total = sums[where].astype(F32) + buffer[chunk, 0].astype(F32) + buffer[chunk, 1].astype(F32)
        sums[where] = total.astype(BF16)
        rs_start(chunk, path, 2)

    def rs_finish(chunk, path):
        rs_wait(chunk, path, 3)
        here, _ = axes(path, 1)
        buffer = bufs[path][3]
        total = sums[block(chunk, path, here)].astype(F32) + buffer[chunk, 0].astype(F32) + buffer[chunk, 1].astype(F32)
        rows = slice(chunk * SUB, chunk * SUB + SUB)
        cols = lanes[path]
        out[rows, cols] = (total * scale[:, cols] + residual[rows, cols].astype(F32)).astype(BF16)

    def multiply(chunk, path):
        def tile(i, carry):
            at = pl.multiple_of(path * HALF + i * 512, 512)
            left = codes[chunk].reshape(DP * PIECE, WIDTH)
            product = jnp.dot(left, weights[:, pl.ds(at, 512)], preferred_element_type=F32)
            sums[chunk, :, :, :, pl.ds(at, 512)] = product.astype(BF16).reshape(RING, RING, SUB, 512)
            return carry

        lax.fori_loop(0, HALF // 512, tile, 0)

    send_own(0)
    send_own(1)
    for i in (2, 3, 4):
        loads()[i].wait()
    for chunk in range(CHUNKS + 1):
        live, late = chunk < CHUNKS, chunk > 0
        if live:
            for kind in range(2):
                y_copy(chunk, kind, True).wait_recv()
                y_copy(chunk, kind + 2, False).start()
                pair_copy(chunk, kind + 1, False).start()
            if chunk + 2 < CHUNKS:
                send_own(chunk + 2)
        if late:
            for path in range(2):
                rs_second(chunk - 1, path, 0)
        if live:
            for kind in range(2):
                y_copy(chunk, kind + 2, True).wait_recv()
                pair_copy(chunk, kind + 3, False).start()
        if late:
            for path in range(2):
                rs_third(chunk - 1, path)
        if live:
            for kind in range(5):
                pair_copy(chunk, kind, True).wait_recv()
            multiply(chunk, 0)
            rs_start(chunk, 0, 0)
        if late:
            for path in range(2):
                rs_second(chunk - 1, path, 1)
        if live:
            multiply(chunk, 1)
            rs_start(chunk, 1, 0)
        if late:
            for path in range(2):
                rs_finish(chunk - 1, path)
    for chunk in range(CHUNKS):
        for kind in range(4):
            y_copy(chunk, kind, False).wait_send()
        for kind in range(5):
            pair_copy(chunk, kind, False).wait_send()
        for path in range(2):
            for step in range(4):
                for way in range(2):
                    rs_copy(chunk, path, step, way).wait_send()


def shards(hidden, exponents, weight_levels, column_scale, residual):
    wide = np.kron(sylvester(32), paley_table()).astype(ml_dtypes.bfloat16)
    anywhere = pl.BlockSpec(memory_space=pl.ANY)
    dma = pltpu.SemaphoreType.DMA

    def vmem(*shape, dtype=BF16):
        return pltpu.VMEM(shape, dtype)

    return pl.pallas_call(
        kernel,
        out_shape=jax.ShapeDtypeStruct(residual.shape, BF16),
        in_specs=[pl.BlockSpec(memory_space=pltpu.SMEM)] + [anywhere] * 5,
        out_specs=pl.BlockSpec(memory_space=pltpu.VMEM),
        scratch_shapes=[
            vmem(ROWS, WIDTH), vmem(WIDE, WIDE), vmem(WIDTH, COLS), vmem(1, COLS, dtype=F32), vmem(ROWS // 2, COLS),
            *[vmem(TENSOR, 16, WIDE) for _ in range(4)],
            vmem(CHUNKS, DP, PIECE, WIDTH), vmem(CHUNKS, RING, RING, SUB, COLS),
            *[
                vmem(CHUNKS, 2, *shape)
                for _ in range(2)
                for shape in ((2, SUB, HALF), (RING, SUB, HALF), (SUB, HALF // 2), (SUB, HALF))
            ],
            dma((5,)), dma((TENSOR,)), dma((TENSOR,)), dma((TENSOR,)), dma((TENSOR,)), dma((2,)),
            dma((CHUNKS, 4)), dma((CHUNKS, 4)), dma((CHUNKS, 5)), dma((CHUNKS, 5)),
            dma((CHUNKS, 16)), dma((CHUNKS, 16)),
        ],
        compiler_params=pltpu.CompilerParams(
            collective_id=0, has_side_effects=True, vmem_limit_bytes=60 * 1024 * 1024,
        ),
        cost_estimate=pl.CostEstimate(flops=15_400_000_000, bytes_accessed=21_000_000, transcendentals=0),
    )(exponents, hidden, wide, weight_levels, column_scale.reshape(1, COLS), residual)


def solution(mesh):
    return jax.shard_map(
        shards,
        mesh=mesh,
        in_specs=(P("dp", "tensor"), P("dp"), P("tensor", "dp"), P("dp"), P("tensor", "dp")),
        out_specs=P("tensor", "dp"),
        check_vma=False,
    )
```

time: 330 us -> 117 us (0.35)
  waiting for transfers between devices: 272 us -> 0 us
  Pallas kernels: 0 us -> 115 us
  matrix products: 22.6 us -> 0 us
  between operations: 13.5 us -> 0.01 us
  starting transfers between devices: 11.1 us -> 0 us
  other arithmetic: 7.56 us -> 0 us
    ppermute x4 -> x0, waiting for transfers between devices: 144 us -> none  [partner_2(): return lax.ppermute(value, axis, pairs)]
    pallas_call x0 -> x1, Pallas kernels: none -> 115 us  [shards(): pl.pallas_call(kernel, out_shape=jax.ShapeDtypeStruct(residual.shape, BF1...]
    reduce_scatter x1 -> x0, waiting for transfers between devices: 79 us -> none  [shards(): lax.psum_scatter(partial_value.astype(jnp.bfloat16), 'tensor', scatter_di...]
    all_gather x1 -> x0, waiting for transfers between devices: 49 us -> none  [shards(): lax.all_gather(flat_rows, 'dp', axis=0, tiled=True)]
    dot_general x3 -> x0, matrix products: 22.6 us -> none  [the longest x1 20 us: shards(): jnp.dot(lax.all_gather(flat_rows, 'dp', axis=0, tiled=True), weight_level...]
    ppermute x4 -> x0, starting transfers between devices: 11 us -> none  [partner_2(): return lax.ppermute(value, axis, pairs)]
    select_n x3 -> x0, other arithmetic: 5.4 us -> none  [shards(): rotated = jnp.where(upper_half, partner - rotated, partner + rotated)]
  transfers between devices with their start and end apart: 6 -> 0, of which waited for: 6 -> 0; matrix products, arithmetic and copies ran while one was open for 0% -> 0% of each run, Pallas kernels for 0% -> 0%
where the time goes in v1:
time: 117 us
  Pallas kernels  115 us (98%)
  local copies, waits for them, and re-layouts  1.67 us (1%)
    pallas_call x1, Pallas kernels, shards(): pl.pallas_call(kernel, out_shape=jax.ShapeDtypeStruct(residual.shape, BF1...  115 us

profile of v1, /device:TPU:0, one launch (start us, length us, event | category | flops | bytes accessed | tf_op | source)
XLA Modules:
  0.0 117.0 jit_solution(6416657000061639948)
XLA Ops:
  0.0 115.3 %shard_map.64 = bf16[64,2048]{1,0:T(8,128)(2,1)} custom-call(s32[128]{0:T(128)} %exponents.1, bf16[128,3328]{1,0:T(8,128)(2,1)} %hidden_hbm.1, bf16[1664,1664]{1,0:T(8,128)(2,1)} %constant.2.clone.wide_hbm, bf16[3328,2048]{1,0:T(8,128)(2,1)} %weights_hbm.1, f32[1,2048]{1,0:T(1,128)} %bitcast.1, bf16[64,2048]{1,0:T(8,128)(2,1)} %residual_hbm.1), custom_call_target="tpu_custom_call" | custom-call | flops 15399999488 | bytes 21000000 | tf_op jit(solution)/shard_map/pallas_call | solution.py:364
  115.3 1.7 %copy.8 = bf16[64,2048]{1,0:T(8,128)(2,1)} copy(bf16[64,2048]{1,0:T(8,128)(2,1)} %shard_map.64) | data formatting | bytes 524288

commit v2 on v1

v2 whole, which is shorter than its diff:
```python
import math

import jax
import jax.numpy as jnp
import ml_dtypes
import numpy as np
from jax import lax
from jax.experimental import pallas as pl
from jax.experimental.pallas import tpu as pltpu
from jax.sharding import PartitionSpec as P

FF = 53248
HAD_SMALL = 52
WIDE = 1664
DP, TENSOR, RING = 8, 16, 4
ROWS = 128
WIDTH = 2 * WIDE
COLS = 2048
HALF = COLS // 2
CHUNKS = 4
PIECE = ROWS // CHUNKS
SUB = PIECE // 2
F32, BF16 = jnp.float32, jnp.bfloat16


def paley_table():
    members = [(a, b) for a in range(5) for b in range(5)]
    squares = set()
    for a, b in members:
        if (a, b) != (0, 0):
            squares.add(((a * a + 2 * b * b) % 5, 2 * a * b % 5))
    jacobsthal = np.zeros((25, 25))
    for i, (a, b) in enumerate(members):
        for j, (c, d) in enumerate(members):
            difference = ((a - c) % 5, (b - d) % 5)
            if difference != (0, 0):
                jacobsthal[i, j] = 1.0 if difference in squares else -1.0
    conference = np.zeros((26, 26))
    conference[0, 1:] = 1.0
    conference[1:, 0] = 1.0
    conference[1:, 1:] = jacobsthal
    hadamard = np.kron(conference, np.array([[1.0, -1.0], [-1.0, -1.0]]))
    return hadamard + np.kron(np.eye(26), np.array([[1.0, 1.0], [1.0, -1.0]]))


def sylvester(count):
    table = np.ones((1, 1))
    while table.shape[0] < count:
        table = np.kron(np.array([[1.0, 1.0], [1.0, -1.0]]), table)
    return table


def kernel(
    exponents_hbm, hidden_hbm, wide_hbm, weights_hbm, scale_hbm, residual_hbm, out,
    exponents, hidden, wide, weights, scale, residual,
    stage, got, stage_back, got_back, codes, sums,
    a1, a2, a3, b1, b2, b3,
    load_sem, out_send, out_recv, back_send, back_recv, own_sem,
    y_send, y_recv, pair_send, pair_recv, rs_send, rs_recv,
):
    d, t = lax.axis_index("dp"), lax.axis_index("tensor")
    z, x = lax.div(t, RING), lax.rem(t, RING)
    core = lax.rem(d, 2)

    def loads():
        pairs = [
            (hidden_hbm, hidden), (wide_hbm, wide), (weights_hbm, weights),
            (scale_hbm, scale), (residual_hbm, residual), (exponents_hbm, exponents),
        ]
        return [pltpu.make_async_copy(src, dst, load_sem.at[i]) for i, (src, dst) in enumerate(pairs)]

    for load in loads():
        load.start()

    def dp_device(distance):
        return (lax.rem(d + 2 * distance + DP, DP), t)

    def pair_device():
        return (d + 1 - 2 * core, t)

    def plane_device(dz, dx):
        return (d, lax.rem(z + dz + RING, RING) * RING + lax.rem(x + dx + RING, RING))

    def offset_device(off):
        return plane_device(lax.div(off, RING), lax.rem(off, RING))

    def offset_source(off):
        return plane_device(-lax.div(off, RING), -lax.rem(off, RING))

    barrier = pltpu.get_barrier_semaphore()

    def greet(off, carry):
        pl.semaphore_signal(barrier, inc=1, device_id=offset_device(off), device_id_type=pl.DeviceIdType.MESH)
        return carry

    lax.fori_loop(1, TENSOR, greet, 0)
    for device in (dp_device(1), dp_device(-1), pair_device()):
        pl.semaphore_signal(barrier, inc=1, device_id=device, device_id_type=pl.DeviceIdType.MESH)

    def remote(src, dst, send, recv, device):
        return pltpu.make_async_remote_copy(
            src_ref=src, dst_ref=dst, send_sem=send, recv_sem=recv,
            device_id=device, device_id_type=pl.DeviceIdType.MESH,
        )

    def holder(chunk, side, i):
        return RING * (chunk % 2 * 2 + side) + 2 * i + (side + chunk // 2) % 2

    odd = lax.rem(z + x, 2)
    first_row = lax.rem(z, 2) * 64 + (2 * odd + lax.div(z, 2)) * 16 + lax.div(x, 2) * 8

    def split(chunk):
        for side in range(2):
            block = hidden[side * 64 + chunk * 16 : side * 64 + chunk * 16 + 16, :].astype(F32)
            for i in range(2):
                rows = block[8 * i : 8 * i + 8]
                stage[holder(chunk, side, i)] = jnp.concatenate([rows[:, :WIDE], rows[:, WIDE:]], axis=0).astype(BF16)

    def out_copy(off):
        device = offset_device(off)
        return remote(stage.at[device[1]], got.at[t], out_send.at[off], out_recv.at[off], device)

    def out_begin(parity):
        turn = lax.rem(odd + parity, 2)

        def begin(i, carry):
            dz = lax.div(i, 2)
            out_copy(RING * dz + 2 * lax.rem(i, 2) + lax.rem(dz + turn, 2)).start()
            return carry

        lax.fori_loop(1 - turn, 8, begin, 0)

    loads()[0].wait()
    split(0)
    split(1)
    pl.semaphore_wait(barrier, TENSOR - 1 + 3)
    out_begin(0)
    split(2)
    split(3)
    out_begin(1)
    mine = pltpu.make_async_copy(stage.at[t], got.at[t], own_sem.at[0])
    mine.start()
    mine.wait()

    def out_wait(off, carry):
        sender = offset_source(off)[1]
        remote(stage.at[t], got.at[sender], out_send.at[off], out_recv.at[off], offset_device(off)).wait_recv()
        return carry

    lax.fori_loop(1, TENSOR, out_wait, 0)
    loads()[1].wait()
    loads()[5].wait()

    row = lax.broadcasted_iota(jnp.int32, (8, 1), 0)
    exponent = jnp.zeros((8, 1), jnp.int32)
    for r in range(8):
        exponent = jnp.where(row == r, exponents[first_row + r], exponent)
    power = jnp.left_shift(1, exponent + 3).astype(F32) * 0.125
    low, high = power * -8.0, power * 7.0

    def transform(at, size):
        left = got[...].reshape(TENSOR * 16, WIDE)
        product = jnp.dot(left, wide[:, pl.ds(at, size)], preferred_element_type=F32)
        parts = [product[8 * i : 8 * i + 8] for i in range(2 * TENSOR)]
        step = 1
        while step < len(parts):
            for i in range(len(parts)):
                if i & step == 0:
                    u, v = parts[i], parts[i + step]
                    parts[i], parts[i + step] = u + v, u - v
            step *= 2
        parts = [jnp.minimum(jnp.maximum(p * (1.0 / math.sqrt(FF)), low), high) for p in parts]
        for i in range(TENSOR):
            stage_back[i, :, pl.ds(at, size)] = jnp.concatenate(parts[2 * i : 2 * i + 2], axis=0).astype(BF16)

    spans = ((0, 768), (768, WIDE - 768))

    def back_copy(piece, off):
        device = offset_device(off)
        lanes = pl.ds(*spans[piece])
        return remote(
            stage_back.at[device[1], :, lanes], got_back.at[t, :, lanes],
            back_send.at[piece, off], back_recv.at[piece, off], device,
        )

    for piece in range(2):
        begin, size = spans[piece]

        def transform_step(i, carry):
            transform(pl.multiple_of(begin + i * 256, 256), 256)
            return carry

        lax.fori_loop(0, size // 256, transform_step, 0)
        if size % 256:
            transform(begin + size // 256 * 256, size % 256)

        def back_begin(off, carry):
            back_copy(piece, off).start()
            return carry

        lax.fori_loop(1, TENSOR, back_begin, 0)
        lanes = pl.ds(begin, size)
        pltpu.make_async_copy(stage_back.at[t, :, lanes], got_back.at[t, :, lanes], own_sem.at[1 + piece]).start()

    for piece in range(2):
        lanes = pl.ds(*spans[piece])
        pltpu.make_async_copy(stage_back.at[t, :, lanes], got_back.at[t, :, lanes], own_sem.at[1 + piece]).wait()

    def back_wait(sender):
        off = lax.rem(z - sender // RING + RING, RING) * RING + lax.rem(x - sender % RING + RING, RING)

        @pl.when(off > 0)
        def _():
            for piece in range(2):
                lanes = pl.ds(*spans[piece])
                remote(
                    stage_back.at[t, :, lanes], got_back.at[sender, :, lanes],
                    back_send.at[piece, off], back_recv.at[piece, off], offset_device(off),
                ).wait_recv()

    def collect(chunk):
        for side in range(2):
            senders = [holder(chunk, side, i) for i in range(2)]
            for sender in senders:
                back_wait(sender)
            blocks = [got_back[sender].astype(F32) for sender in senders]
            for half in range(2):
                rows = jnp.concatenate([b[8 * half : 8 * half + 8] for b in blocks], axis=0)
                codes[chunk, d, side * SUB : side * SUB + SUB, half * WIDE : half * WIDE + WIDE] = rows.astype(BF16)
        pair_copy(chunk, 0, False).start()

    def index(distance):
        return lax.rem(d + 2 * distance + DP, DP)

    def whole(chunk, distance):
        return codes.at[chunk, index(distance)]

    def part(chunk, distance, side):
        return codes.at[chunk, index(distance), side * SUB : side * SUB + SUB]

    def y_copy(chunk, kind, receiving):
        sign = 1 if kind in (0, 2) else -1
        if kind < 2:
            ref = whole(chunk, -sign if receiving else 0)
        else:
            ref = part(chunk, -2 * sign if receiving else -sign, kind - 2)
        return remote(ref, ref, y_send.at[chunk, kind], y_recv.at[chunk, kind], dp_device(sign))

    def pair_copy(chunk, kind, receiving):
        def ref_of(base):
            if kind < 3:
                return codes.at[chunk, lax.rem(base + 2 * (0, -1, 1)[kind] + DP, DP)]
            return codes.at[chunk, lax.rem(base + 4, DP), (kind - 3) * SUB : (kind - 3) * SUB + SUB]

        ref = ref_of(pair_device()[0] if receiving else d)
        return remote(ref, ref, pair_send.at[chunk, kind], pair_recv.at[chunk, kind], pair_device())

    def send_own(chunk):
        for kind in range(2):
            y_copy(chunk, kind, False).start()

    lanes = (slice(0, HALF), slice(HALF, COLS))
    bufs = ((a1, a2, a3), (b1, b2, b3))

    def group(chunk, path, target, side=None):
        span = slice(None) if side is None else slice(2 * side, 2 * side + 2)
        if path == 0:
            return (chunk, target, span, slice(None), lanes[path])
        return (chunk, span, target, slice(None), lanes[path])

    def block(chunk, path, target):
        where = (z, target) if path == 0 else (target, x)
        return (chunk, *where, slice(None), lanes[path])

    def axes(path, phase):
        along_z = (path == 0) == (phase == 0)
        if along_z:
            return z, lambda n: plane_device(n, 0)
        return x, lambda n: plane_device(0, n)

    def rs_copy(chunk, path, step, way):
        sign = (1, -1, 2)[way]
        here, device = axes(path, step // 2)
        target = lax.rem(here + (2 if step == 0 else sign) + RING, RING)
        if step == 0:
            src = sums.at[group(chunk, path, target, way)]
        elif step == 1:
            src = sums.at[group(chunk, path, target)]
        else:
            src = sums.at[block(chunk, path, target)]
        number = path * 7 + step * 2 + way
        return remote(
            src, bufs[path][step].at[chunk, way],
            rs_send.at[chunk, number], rs_recv.at[chunk, number], device(sign),
        )

    def rs_start(chunk, path, step):
        for way in range(3 if step == 2 else 2):
            rs_copy(chunk, path, step, way).start()

    def rs_second(chunk, path):
        here, _ = axes(path, 0)
        for way in range(2):
            rs_copy(chunk, path, 0, way).wait_recv()
            where = group(chunk, path, lax.rem(here + (1, -1)[way] + RING, RING), way)
            sums[where] = (sums[where].astype(F32) + bufs[path][0][chunk, way].astype(F32)).astype(BF16)
            rs_copy(chunk, path, 1, way).start()

    def rs_third(chunk, path):
        where = group(chunk, path, axes(path, 0)[0])
        total = sums[where].astype(F32)
        for way in range(2):
            rs_copy(chunk, path, 1, way).wait_recv()
            total += bufs[path][1][chunk, way].astype(F32)
        sums[where] = total.astype(BF16)
        rs_start(chunk, path, 2)

    def rs_finish(chunk, path):
        total = sums[block(chunk, path, axes(path, 1)[0])].astype(F32)
        for way in range(3):
            rs_copy(chunk, path, 2, way).wait_recv()
            total += bufs[path][2][chunk, way].astype(F32)
        rows, cols = slice(chunk * SUB, chunk * SUB + SUB), lanes[path]
        out[rows, cols] = (total * scale[:, cols] + residual[rows, cols].astype(F32)).astype(BF16)

    height = lax.div(d, 2)

    def multiply_own(path):
        def tile(i, carry):
            at = pl.multiple_of(path * HALF + i * 512, 512)
            left = codes[:, pl.ds(2 * height, 2)].reshape(CHUNKS * 2 * PIECE, WIDTH)
            product = jnp.dot(left, weights[:, pl.ds(at, 512)], preferred_element_type=F32)
            sums[:, height, :, :, pl.ds(at, 512)] = product.astype(BF16).reshape(CHUNKS, RING, SUB, 512)
            return carry

        lax.fori_loop(0, HALF // 512, tile, 0)

    def multiply(chunk, path):
        others = [lax.rem(height + i, RING) for i in range(1, RING)]

        def tile(i, carry):
            at = pl.multiple_of(path * HALF + i * 512, 512)
            left = jnp.concatenate([codes[chunk, pl.ds(2 * o, 2)].reshape(2 * PIECE, WIDTH) for o in others], axis=0)
            product = jnp.dot(left, weights[:, pl.ds(at, 512)], preferred_element_type=F32).astype(BF16)
            for j, o in enumerate(others):
                rows = product[j * 2 * PIECE : (j + 1) * 2 * PIECE]
                sums[chunk, o, :, :, pl.ds(at, 512)] = rows.reshape(RING, SUB, 512)
            return carry

        lax.fori_loop(0, HALF // 512, tile, 0)

    def near(chunk):
        for kind in range(2):
            y_copy(chunk, kind, True).wait_recv()
            y_copy(chunk, kind + 2, False).start()
            pair_copy(chunk, kind + 1, False).start()

    def far(chunk):
        for kind in range(2):
            y_copy(chunk, kind + 2, True).wait_recv()
            pair_copy(chunk, kind + 3, False).start()

    def own(path):
        if path == 0:
            for i in (2, 3, 4):
                loads()[i].wait()
            for chunk in range(CHUNKS):
                pair_copy(chunk, 0, True).wait_recv()
        multiply_own(path)

    def product(chunk, path):
        if path == 0:
            for kind in range(1, 5):
                pair_copy(chunk, kind, True).wait_recv()
        multiply(chunk, path)
        rs_start(chunk, path, 0)

    def reduce(chunk, path, step):
        (rs_second, rs_third, None, rs_finish)[step - 2](chunk, path)

    collect(0)
    send_own(0)
    collect(1)
    collect(2)
    collect(3)
    send_own(1)
    near(0)
    own(0)
    send_own(2)
    own(1)
    near(1)
    send_own(3)
    far(0)
    product(0, 0)
    product(0, 1)
    near(2)
    far(1)
    reduce(0, 0, 2)
    reduce(0, 1, 2)
    product(1, 0)
    product(1, 1)
    near(3)
    reduce(0, 0, 3)
    reduce(0, 1, 3)
    far(2)
    reduce(1, 0, 2)
    reduce(1, 1, 2)
    product(2, 0)
    far(3)
    product(2, 1)
    product(3, 0)
    reduce(1, 0, 3)
    product(3, 1)
    reduce(2, 0, 2)
    reduce(2, 1, 2)
    reduce(3, 0, 2)
    reduce(3, 1, 2)
    reduce(1, 1, 3)
    reduce(2, 1, 3)
    reduce(1, 0, 5)
    reduce(2, 0, 3)
    reduce(0, 1, 5)
    reduce(0, 0, 5)
    reduce(3, 0, 3)
    reduce(3, 1, 3)
    reduce(2, 1, 5)
    reduce(1, 1, 5)
    reduce(2, 0, 5)
    reduce(3, 0, 5)
    reduce(3, 1, 5)

    def drain(off, carry):
        out_copy(off).wait_send()
        for piece in range(2):
            back_copy(piece, off).wait_send()
        return carry

    lax.fori_loop(1, TENSOR, drain, 0)
    for chunk in range(CHUNKS):
        for kind in range(4):
            y_copy(chunk, kind, False).wait_send()
        for kind in range(5):
            pair_copy(chunk, kind, False).wait_send()
        for path in range(2):
            for step in range(3):
                for way in range(3 if step == 2 else 2):
                    rs_copy(chunk, path, step, way).wait_send()


def shards(hidden, exponents, weight_levels, column_scale, residual):
    wide = np.kron(sylvester(32), paley_table()).astype(ml_dtypes.bfloat16)
    anywhere = pl.BlockSpec(memory_space=pl.ANY)
    dma = pltpu.SemaphoreType.DMA

    def vmem(*shape, dtype=BF16):
        return pltpu.VMEM(shape, dtype)

    return pl.pallas_call(
        kernel,
        out_shape=jax.ShapeDtypeStruct(residual.shape, BF16),
        in_specs=[anywhere] * 6,
        out_specs=pl.BlockSpec(memory_space=pltpu.VMEM),
        scratch_shapes=[
            pltpu.SMEM((ROWS,), jnp.int32), vmem(ROWS, WIDTH), vmem(WIDE, WIDE), vmem(WIDTH, COLS), vmem(1, COLS, dtype=F32), vmem(ROWS // 2, COLS),
            *[vmem(TENSOR, 16, WIDE) for _ in range(4)],
            vmem(CHUNKS, DP, PIECE, WIDTH), vmem(CHUNKS, RING, RING, SUB, COLS),
            *[
                vmem(CHUNKS, *shape)
                for _ in range(2)
                for shape in ((2, 2, SUB, HALF), (2, RING, SUB, HALF), (3, SUB, HALF))
            ],
            dma((6,)), dma((TENSOR,)), dma((TENSOR,)), dma((2, TENSOR)), dma((2, TENSOR)), dma((3,)),
            dma((CHUNKS, 4)), dma((CHUNKS, 4)), dma((CHUNKS, 5)), dma((CHUNKS, 5)),
            dma((CHUNKS, 14)), dma((CHUNKS, 14)),
        ],
        compiler_params=pltpu.CompilerParams(
            collective_id=0, has_side_effects=True, vmem_limit_bytes=60 * 1024 * 1024,
        ),
        cost_estimate=pl.CostEstimate(flops=15_400_000_000, bytes_accessed=21_000_000, transcendentals=0),
    )(exponents, hidden, wide, weight_levels, column_scale.reshape(1, COLS), residual)


def solution(mesh):
    return jax.shard_map(
        shards,
        mesh=mesh,
        in_specs=(P("dp", "tensor"), P("dp"), P("tensor", "dp"), P("dp"), P("tensor", "dp")),
        out_specs=P("tensor", "dp"),
        check_vma=False,
    )
```

time: 117 us -> 87.9 us (0.75)
  Pallas kernels: 115 us -> 86.1 us
    pallas_call x1, Pallas kernels: 115 us -> 86.1 us  [shards(): pl.pallas_call(kernel, out_shape=jax.ShapeDtypeStruct(residual.shape, BF1...]
where the time goes in v2:
time: 87.9 us; the launch traced here: 87.8 us
  Pallas kernels  86.1 us (98%)
  local copies, waits for them, and re-layouts  1.67 us (2%)
    pallas_call x1, Pallas kernels, shards(): pl.pallas_call(kernel, out_shape=jax.ShapeDtypeStruct(residual.shape, BF1...  86.1 us

profile of v2, /device:TPU:0, one launch (start us, length us, event | category | flops | bytes accessed | tf_op | source)
XLA Modules:
  0.0 87.8 jit_solution(1806754621402806159)
XLA Ops:
  0.0 86.1 %shard_map.64 = bf16[64,2048]{1,0:T(8,128)(2,1)} custom-call(s32[128]{0:T(128)} %exponents_hbm.1, bf16[128,3328]{1,0:T(8,128)(2,1)} %hidden_hbm.1, bf16[1664,1664]{1,0:T(8,128)(2,1)} %constant.2.clone.wide_hbm, bf16[3328,2048]{1,0:T(8,128)(2,1)} %weights_hbm.1, f32[1,2048]{1,0:T(1,128)} %bitcast.1, bf16[64,2048]{1,0:T(8,128)(2,1)} %residual_hbm.1), custom_call_target="tpu_custom_call" | custom-call | flops 15399999488 | bytes 21000000 | tf_op jit(solution)/shard_map/pallas_call | solution.py:458
  86.1 1.7 %copy.8 = bf16[64,2048]{1,0:T(8,128)(2,1)} copy(bf16[64,2048]{1,0:T(8,128)(2,1)} %shard_map.64) | data formatting | bytes 524288

commit v3 on v2

--- a/solution.py
+++ b/solution.py
@@ -16,7 +16,8 @@
 ROWS = 128
 WIDTH = 2 * WIDE
 COLS = 2048
-HALF = COLS // 2
+PATHS = 2
+PART = COLS // PATHS
 CHUNKS = 4
 PIECE = ROWS // CHUNKS
 SUB = PIECE // 2
@@ -54,7 +55,7 @@
     exponents_hbm, hidden_hbm, wide_hbm, weights_hbm, scale_hbm, residual_hbm, out,
     exponents, hidden, wide, weights, scale, residual,
     stage, got, stage_back, got_back, codes, sums,
-    a1, a2, a3, b1, b2, b3,
+    arrived_1, arrived_2, arrived_3,
     load_sem, out_send, out_recv, back_send, back_recv, own_sem,
     y_send, y_recv, pair_send, pair_recv, rs_send, rs_recv,
 ):
@@ -69,33 +70,28 @@
         ]
         return [pltpu.make_async_copy(src, dst, load_sem.at[i]) for i, (src, dst) in enumerate(pairs)]
 
+    def dp_device(distance):
+        return (lax.rem(d + 2 * distance + DP, DP), t)
+
+    def pair_device():
+        return (d + 1 - 2 * core, t)
+
+    def plane_device(dz, dx):
+        return (d, lax.rem(z + dz + RING, RING) * RING + lax.rem(x + dx + RING, RING))
+
+    def offset_device(off):
+        return plane_device(lax.div(off, RING), lax.rem(off, RING))
+
+    def offset_source(off):
+        return plane_device(-lax.div(off, RING), -lax.rem(off, RING))
+
+    barrier = pltpu.get_barrier_semaphore()
+
+    far_first = sorted(range(1, TENSOR), key=lambda off: -(min(off // RING, RING - off // RING) + min(off % RING, RING - off % RING)))
+    for device in [plane_device(off // RING, off % RING) for off in far_first] + [dp_device(1), dp_device(-1), pair_device()]:
+        pl.semaphore_signal(barrier, inc=1, device_id=device, device_id_type=pl.DeviceIdType.MESH)
     for load in loads():
         load.start()
-
-    def dp_device(distance):
-        return (lax.rem(d + 2 * distance + DP, DP), t)
-
-    def pair_device():
-        return (d + 1 - 2 * core, t)
-
-    def plane_device(dz, dx):
-        return (d, lax.rem(z + dz + RING, RING) * RING + lax.rem(x + dx + RING, RING))
-
-    def offset_device(off):
-        return plane_device(lax.div(off, RING), lax.rem(off, RING))
-
-    def offset_source(off):
-        return plane_device(-lax.div(off, RING), -lax.rem(off, RING))
-
-    barrier = pltpu.get_barrier_semaphore()
-
-    def greet(off, carry):
-        pl.semaphore_signal(barrier, inc=1, device_id=offset_device(off), device_id_type=pl.DeviceIdType.MESH)
-        return carry
-
-    lax.fori_loop(1, TENSOR, greet, 0)
-    for device in (dp_device(1), dp_device(-1), pair_device()):
-        pl.semaphore_signal(barrier, inc=1, device_id=device, device_id_type=pl.DeviceIdType.MESH)
 
     def remote(src, dst, send, recv, device):
         return pltpu.make_async_remote_copy(
@@ -239,11 +235,9 @@
         return codes.at[chunk, index(distance), side * SUB : side * SUB + SUB]
 
     def y_copy(chunk, kind, receiving):
-        sign = 1 if kind in (0, 2) else -1
-        if kind < 2:
-            ref = whole(chunk, -sign if receiving else 0)
-        else:
-            ref = part(chunk, -2 * sign if receiving else -sign, kind - 2)
+        sign = -1 if kind % 2 else 1
+        distance = -sign if kind in (2, 3) else 0
+        ref = part(chunk, distance - sign if receiving else distance, kind % 2 if kind < 4 else 5 - kind)
         return remote(ref, ref, y_send.at[chunk, kind], y_recv.at[chunk, kind], dp_device(sign))
 
     def pair_copy(chunk, kind, receiving):
@@ -256,24 +250,23 @@
         return remote(ref, ref, pair_send.at[chunk, kind], pair_recv.at[chunk, kind], pair_device())
 
     def send_own(chunk):
-        for kind in range(2):
+        for kind in (0, 1, 4, 5):
             y_copy(chunk, kind, False).start()
 
-    lanes = (slice(0, HALF), slice(HALF, COLS))
-    bufs = ((a1, a2, a3), (b1, b2, b3))
+    def z_first(path):
+        return path < PATHS // 2
+
+    lanes = [slice(path * PART, path * PART + PART) for path in range(PATHS)]
+    bufs = (arrived_1, arrived_2, arrived_3)
 
     def group(chunk, path, target, side=None):
-        span = slice(None) if side is None else slice(2 * side, 2 * side + 2)
-        if path == 0:
-            return (chunk, target, span, slice(None), lanes[path])
-        return (chunk, span, target, slice(None), lanes[path])
+        return (chunk, path, target, slice(None) if side is None else slice(2 * side, 2 * side + 2))
 
     def block(chunk, path, target):
-        where = (z, target) if path == 0 else (target, x)
-        return (chunk, *where, slice(None), lanes[path])
+        return (chunk, path, z if z_first(path) else x, target)
 
     def axes(path, phase):
-        along_z = (path == 0) == (phase == 0)
+        along_z = z_first(path) == (phase == 0)
         if along_z:
             return z, lambda n: plane_device(n, 0)
         return x, lambda n: plane_device(0, n)
@@ -290,7 +283,7 @@
             src = sums.at[block(chunk, path, target)]
         number = path * 7 + step * 2 + way
         return remote(
-            src, bufs[path][step].at[chunk, way],
+            src, bufs[step].at[chunk, path, way],
             rs_send.at[chunk, number], rs_recv.at[chunk, number], device(sign),
         )
 
@@ -303,7 +296,7 @@
         for way in range(2):
             rs_copy(chunk, path, 0, way).wait_recv()
             where = group(chunk, path, lax.rem(here + (1, -1)[way] + RING, RING), way)
-            sums[where] = (sums[where].astype(F32) + bufs[path][0][chunk, way].astype(F32)).astype(BF16)
+            sums[where] = (sums[where].astype(F32) + bufs[0][chunk, path, way].astype(F32)).astype(BF16)
             rs_copy(chunk, path, 1, way).start()
 
     def rs_third(chunk, path):
@@ -311,7 +304,7 @@
         total = sums[where].astype(F32)
         for way in range(2):
             rs_copy(chunk, path, 1, way).wait_recv()
-            total += bufs[path][1][chunk, way].astype(F32)
+            total += bufs[1][chunk, path, way].astype(F32)
         sums[where] = total.astype(BF16)
         rs_start(chunk, path, 2)
 
@@ -319,7 +312,7 @@
         total = sums[block(chunk, path, axes(path, 1)[0])].astype(F32)
         for way in range(3):
             rs_copy(chunk, path, 2, way).wait_recv()
-            total += bufs[path][2][chunk, way].astype(F32)
+            total += bufs[2][chunk, path, way].astype(F32)
         rows, cols = slice(chunk * SUB, chunk * SUB + SUB), lanes[path]
         out[rows, cols] = (total * scale[:, cols] + residual[rows, cols].astype(F32)).astype(BF16)
 
@@ -327,32 +320,43 @@
 
     def multiply_own(path):
         def tile(i, carry):
-            at = pl.multiple_of(path * HALF + i * 512, 512)
+            at = pl.multiple_of(i * 512, 512)
             left = codes[:, pl.ds(2 * height, 2)].reshape(CHUNKS * 2 * PIECE, WIDTH)
-            product = jnp.dot(left, weights[:, pl.ds(at, 512)], preferred_element_type=F32)
-            sums[:, height, :, :, pl.ds(at, 512)] = product.astype(BF16).reshape(CHUNKS, RING, SUB, 512)
+            product = jnp.dot(left, weights[:, pl.ds(path * PART + at, 512)], preferred_element_type=F32)
+            rows = product.astype(BF16).reshape(CHUNKS, RING, SUB, 512)
+            if z_first(path):
+                sums[:, path, height, :, :, pl.ds(at, 512)] = rows
+            else:
+                sums[:, path, :, height, :, pl.ds(at, 512)] = rows
             return carry
 
-        lax.fori_loop(0, HALF // 512, tile, 0)
+        lax.fori_loop(0, PART // 512, tile, 0)
 
     def multiply(chunk, path):
         others = [lax.rem(height + i, RING) for i in range(1, RING)]
 
         def tile(i, carry):
-            at = pl.multiple_of(path * HALF + i * 512, 512)
+            at = pl.multiple_of(i * 512, 512)
             left = jnp.concatenate([codes[chunk, pl.ds(2 * o, 2)].reshape(2 * PIECE, WIDTH) for o in others], axis=0)
-            product = jnp.dot(left, weights[:, pl.ds(at, 512)], preferred_element_type=F32).astype(BF16)
+            product = jnp.dot(left, weights[:, pl.ds(path * PART + at, 512)], preferred_element_type=F32).astype(BF16)
             for j, o in enumerate(others):
-                rows = product[j * 2 * PIECE : (j + 1) * 2 * PIECE]
-                sums[chunk, o, :, :, pl.ds(at, 512)] = rows.reshape(RING, SUB, 512)
+                rows = product[j * 2 * PIECE : (j + 1) * 2 * PIECE].reshape(RING, SUB, 512)
+                if z_first(path):
+                    sums[chunk, path, o, :, :, pl.ds(at, 512)] = rows
+                else:
+                    sums[chunk, path, :, o, :, pl.ds(at, 512)] = rows
             return carry
 
-        lax.fori_loop(0, HALF // 512, tile, 0)
+        lax.fori_loop(0, PART // 512, tile, 0)
 
     def near(chunk):
         for kind in range(2):
             y_copy(chunk, kind, True).wait_recv()
             y_copy(chunk, kind + 2, False).start()
+
+    def rest(chunk):
+        for kind in range(2):
+            y_copy(chunk, kind + 4, True).wait_recv()
             pair_copy(chunk, kind + 1, False).start()
 
     def far(chunk):
@@ -378,73 +382,82 @@
     def reduce(chunk, path, step):
         (rs_second, rs_third, None, rs_finish)[step - 2](chunk, path)
 
+    def drain(off, carry):
+        out_copy(off).wait_send()
+        for piece in range(2):
+            back_copy(piece, off).wait_send()
+        return carry
+
+    def sent(chunk):
+        for kind in range(6):
+            y_copy(chunk, kind, False).wait_send()
+        for kind in range(5):
+            pair_copy(chunk, kind, False).wait_send()
+
+    def passed(chunk, steps):
+        for path in range(PATHS):
+            for step in steps:
+                for way in range(3 if step == 2 else 2):
+                    rs_copy(chunk, path, step, way).wait_send()
+
     collect(0)
     send_own(0)
     collect(1)
     collect(2)
     collect(3)
+    near(0)
+    lax.fori_loop(1, TENSOR, drain, 0)
+    own(0)
     send_own(1)
-    near(0)
-    own(0)
+    own(1)
+    rest(0)
+    far(0)
+    near(1)
     send_own(2)
-    own(1)
-    near(1)
-    send_own(3)
-    far(0)
     product(0, 0)
     product(0, 1)
-    near(2)
+    rest(1)
     far(1)
     reduce(0, 0, 2)
+    near(2)
+    send_own(3)
     reduce(0, 1, 2)
     product(1, 0)
+    rest(2)
     product(1, 1)
+    far(2)
+    reduce(1, 0, 2)
     near(3)
     reduce(0, 0, 3)
     reduce(0, 1, 3)
-    far(2)
-    reduce(1, 0, 2)
+    product(2, 0)
     reduce(1, 1, 2)
-    product(2, 0)
+    rest(3)
+    product(2, 1)
     far(3)
-    product(2, 1)
+    reduce(1, 0, 3)
     product(3, 0)
-    reduce(1, 0, 3)
     product(3, 1)
     reduce(2, 0, 2)
     reduce(2, 1, 2)
     reduce(3, 0, 2)
+    reduce(0, 0, 5)
     reduce(3, 1, 2)
+    reduce(2, 0, 3)
     reduce(1, 1, 3)
+    reduce(1, 0, 5)
     reduce(2, 1, 3)
-    reduce(1, 0, 5)
-    reduce(2, 0, 3)
-    reduce(0, 1, 5)
-    reduce(0, 0, 5)
     reduce(3, 0, 3)
     reduce(3, 1, 3)
+    reduce(1, 1, 5)
+    reduce(0, 1, 5)
     reduce(2, 1, 5)
-    reduce(1, 1, 5)
     reduce(2, 0, 5)
     reduce(3, 0, 5)
     reduce(3, 1, 5)
-
-    def drain(off, carry):
-        out_copy(off).wait_send()
-        for piece in range(2):
-            back_copy(piece, off).wait_send()
-        return carry
-
-    lax.fori_loop(1, TENSOR, drain, 0)
     for chunk in range(CHUNKS):
-        for kind in range(4):
-            y_copy(chunk, kind, False).wait_send()
-        for kind in range(5):
-            pair_copy(chunk, kind, False).wait_send()
-        for path in range(2):
-            for step in range(3):
-                for way in range(3 if step == 2 else 2):
-                    rs_copy(chunk, path, step, way).wait_send()
+        sent(chunk)
+        passed(chunk, (0, 1, 2))
 
 
 def shards(hidden, exponents, weight_levels, column_scale, residual):
@@ -463,15 +476,14 @@
         scratch_shapes=[
             pltpu.SMEM((ROWS,), jnp.int32), vmem(ROWS, WIDTH), vmem(WIDE, WIDE), vmem(WIDTH, COLS), vmem(1, COLS, dtype=F32), vmem(ROWS // 2, COLS),
             *[vmem(TENSOR, 16, WIDE) for _ in range(4)],
-            vmem(CHUNKS, DP, PIECE, WIDTH), vmem(CHUNKS, RING, RING, SUB, COLS),
+            vmem(CHUNKS, DP, PIECE, WIDTH), vmem(CHUNKS, PATHS, RING, RING, SUB, PART),
             *[
-                vmem(CHUNKS, *shape)
-                for _ in range(2)
-                for shape in ((2, 2, SUB, HALF), (2, RING, SUB, HALF), (3, SUB, HALF))
+                vmem(CHUNKS, PATHS, *shape)
+                for shape in ((2, 2, SUB, PART), (2, RING, SUB, PART), (3, SUB, PART))
             ],
             dma((6,)), dma((TENSOR,)), dma((TENSOR,)), dma((2, TENSOR)), dma((2, TENSOR)), dma((3,)),
-            dma((CHUNKS, 4)), dma((CHUNKS, 4)), dma((CHUNKS, 5)), dma((CHUNKS, 5)),
-            dma((CHUNKS, 14)), dma((CHUNKS, 14)),
+            dma((CHUNKS, 6)), dma((CHUNKS, 6)), dma((CHUNKS, 5)), dma((CHUNKS, 5)),
+            dma((CHUNKS, 7 * PATHS)), dma((CHUNKS, 7 * PATHS)),
         ],
         compiler_params=pltpu.CompilerParams(
             collective_id=0, has_side_effects=True, vmem_limit_bytes=60 * 1024 * 1024,

time: 87.9 us -> 86.1 us (0.980)
  Pallas kernels: 86.1 us -> 84.3 us
    pallas_call x1, Pallas kernels: 86.1 us -> 84.3 us  [shards(): pl.pallas_call(kernel, out_shape=jax.ShapeDtypeStruct(residual.shape, BF1...]
where the time goes in v3:
time: 86.1 us; the launch traced here: 85.9 us
  Pallas kernels  84.3 us (98%)
  local copies, waits for them, and re-layouts  1.67 us (2%)
    pallas_call x1, Pallas kernels, shards(): pl.pallas_call(kernel, out_shape=jax.ShapeDtypeStruct(residual.shape, BF1...  84.3 us

profile of v3, /device:TPU:0, one launch (start us, length us, event | category | flops | bytes accessed | tf_op | source)
XLA Modules:
  0.0 85.9 jit_solution(11149882180247322802)
XLA Ops:
  0.0 84.3 %shard_map.64 = bf16[64,2048]{1,0:T(8,128)(2,1)} custom-call(s32[128]{0:T(128)} %exponents_hbm.1, bf16[128,3328]{1,0:T(8,128)(2,1)} %hidden_hbm.1, bf16[1664,1664]{1,0:T(8,128)(2,1)} %constant.2.clone.wide_hbm, bf16[3328,2048]{1,0:T(8,128)(2,1)} %weights_hbm.1, f32[1,2048]{1,0:T(1,128)} %bitcast.1, bf16[64,2048]{1,0:T(8,128)(2,1)} %residual_hbm.1), custom_call_target="tpu_custom_call" | custom-call | flops 15399999488 | bytes 21000000 | tf_op jit(solution)/shard_map/pallas_call | solution.py:471
  84.3 1.7 %copy.8 = bf16[64,2048]{1,0:T(8,128)(2,1)} copy(bf16[64,2048]{1,0:T(8,128)(2,1)} %shard_map.64) | data formatting | bytes 524288

commit v4 on v3

--- a/solution.py
+++ b/solution.py
@@ -52,12 +52,12 @@
 
 
 def kernel(
-    exponents_hbm, hidden_hbm, wide_hbm, weights_hbm, scale_hbm, residual_hbm, out,
+    exponents_hbm, hidden_hbm, wide_hbm, weights_hbm, scale_hbm, residual_hbm, out_hbm,
     exponents, hidden, wide, weights, scale, residual,
     stage, got, stage_back, got_back, codes, sums,
     arrived_1, arrived_2, arrived_3,
     load_sem, out_send, out_recv, back_send, back_recv, own_sem,
-    y_send, y_recv, pair_send, pair_recv, rs_send, rs_recv,
+    y_send, y_recv, pair_send, pair_recv, rs_send, rs_recv, out, write_sem,
 ):
     d, t = lax.axis_index("dp"), lax.axis_index("tensor")
     z, x = lax.div(t, RING), lax.rem(t, RING)
@@ -308,6 +308,10 @@
         sums[where] = total.astype(BF16)
         rs_start(chunk, path, 2)
 
+    def write(chunk, path):
+        where = (slice(chunk * SUB, chunk * SUB + SUB), lanes[path])
+        return pltpu.make_async_copy(out.at[where], out_hbm.at[where], write_sem.at[chunk, path])
+
     def rs_finish(chunk, path):
         total = sums[block(chunk, path, axes(path, 1)[0])].astype(F32)
         for way in range(3):
@@ -315,6 +319,7 @@
             total += bufs[2][chunk, path, way].astype(F32)
         rows, cols = slice(chunk * SUB, chunk * SUB + SUB), lanes[path]
         out[rows, cols] = (total * scale[:, cols] + residual[rows, cols].astype(F32)).astype(BF16)
+        write(chunk, path).start()
 
     height = lax.div(d, 2)
 
@@ -333,21 +338,22 @@
         lax.fori_loop(0, PART // 512, tile, 0)
 
     def multiply(chunk, path):
+        width = PART if chunk == CHUNKS - 1 else 512
         others = [lax.rem(height + i, RING) for i in range(1, RING)]
 
         def tile(i, carry):
-            at = pl.multiple_of(i * 512, 512)
+            at = pl.multiple_of(i * width, width)
             left = jnp.concatenate([codes[chunk, pl.ds(2 * o, 2)].reshape(2 * PIECE, WIDTH) for o in others], axis=0)
-            product = jnp.dot(left, weights[:, pl.ds(path * PART + at, 512)], preferred_element_type=F32).astype(BF16)
+            product = jnp.dot(left, weights[:, pl.ds(path * PART + at, width)], preferred_element_type=F32).astype(BF16)
             for j, o in enumerate(others):
-                rows = product[j * 2 * PIECE : (j + 1) * 2 * PIECE].reshape(RING, SUB, 512)
+                rows = product[j * 2 * PIECE : (j + 1) * 2 * PIECE].reshape(RING, SUB, width)
                 if z_first(path):
-                    sums[chunk, path, o, :, :, pl.ds(at, 512)] = rows
+                    sums[chunk, path, o, :, :, pl.ds(at, width)] = rows
                 else:
-                    sums[chunk, path, :, o, :, pl.ds(at, 512)] = rows
+                    sums[chunk, path, :, o, :, pl.ds(at, width)] = rows
             return carry
 
-        lax.fori_loop(0, PART // 512, tile, 0)
+        lax.fori_loop(0, PART // width, tile, 0)
 
     def near(chunk):
         for kind in range(2):
@@ -458,6 +464,8 @@
     for chunk in range(CHUNKS):
         sent(chunk)
         passed(chunk, (0, 1, 2))
+        for path in range(PATHS):
+            write(chunk, path).wait()
 
 
 def shards(hidden, exponents, weight_levels, column_scale, residual):
@@ -472,7 +480,7 @@
         kernel,
         out_shape=jax.ShapeDtypeStruct(residual.shape, BF16),
         in_specs=[anywhere] * 6,
-        out_specs=pl.BlockSpec(memory_space=pltpu.VMEM),
+        out_specs=anywhere,
         scratch_shapes=[
             pltpu.SMEM((ROWS,), jnp.int32), vmem(ROWS, WIDTH), vmem(WIDE, WIDE), vmem(WIDTH, COLS), vmem(1, COLS, dtype=F32), vmem(ROWS // 2, COLS),
             *[vmem(TENSOR, 16, WIDE) for _ in range(4)],
@@ -484,6 +492,7 @@
             dma((6,)), dma((TENSOR,)), dma((TENSOR,)), dma((2, TENSOR)), dma((2, TENSOR)), dma((3,)),
             dma((CHUNKS, 6)), dma((CHUNKS, 6)), dma((CHUNKS, 5)), dma((CHUNKS, 5)),
             dma((CHUNKS, 7 * PATHS)), dma((CHUNKS, 7 * PATHS)),
+            vmem(ROWS // 2, COLS), dma((CHUNKS, PATHS)),
         ],
         compiler_params=pltpu.CompilerParams(
             collective_id=0, has_side_effects=True, vmem_limit_bytes=60 * 1024 * 1024,

time: 86.1 us -> 85.8 us (level)
  no operation moved by 1% of the time
where the time goes in v4:
time: 85.8 us; the launch traced here: 85.7 us
  Pallas kernels  84 us (98%)
  local copies, waits for them, and re-layouts  1.67 us (2%)
    pallas_call x1, Pallas kernels, shards(): pl.pallas_call(kernel, out_shape=jax.ShapeDtypeStruct(residual.shape, BF1...  84 us

profile of v4, /device:TPU:0, one launch (start us, length us, event | category | flops | bytes accessed | tf_op | source)
XLA Modules:
  0.0 85.7 jit_solution(15306176082079901234)
XLA Ops:
  0.0 84.0 %shard_map.64 = bf16[64,2048]{1,0:T(8,128)(2,1)} custom-call(s32[128]{0:T(128)} %exponents_hbm.1, bf16[128,3328]{1,0:T(8,128)(2,1)} %hidden_hbm.1, bf16[1664,1664]{1,0:T(8,128)(2,1)} %constant.2.clone.wide_hbm, bf16[3328,2048]{1,0:T(8,128)(2,1)} %weights_hbm.1, f32[1,2048]{1,0:T(1,128)} %bitcast.1, bf16[64,2048]{1,0:T(8,128)(2,1)} %residual_hbm.1), custom_call_target="tpu_custom_call" | custom-call | flops 15399999488 | bytes 21000000 | tf_op jit(solution)/shard_map/pallas_call | solution.py:479
  84.0 1.7 %copy.8 = bf16[64,2048]{1,0:T(8,128)(2,1)} copy(bf16[64,2048]{1,0:T(8,128)(2,1)} %shard_map.64) | data formatting | bytes 524288
